TPU v7x, 256 devices: a whole 4x4x8 slice. The times are simulated.
256 devices in a mesh: pb: 16 (over y, z_hi), ka: 16 (over z_lo, x, core).
Axes of the slice: x: 4, y: 4, z: 8 (z_hi: 4, z_lo: 2; z = z_hi * 2 + z_lo), core: 2. Of those that a mesh axis runs over, the one named last changes fastest.
Arguments:
- queries: bfloat16 [16384, 1024], P(('pb', 'ka')), may hold values from -6 to 6
- key_vecs: bfloat16 [16384, 128], P(('pb', 'ka')), may hold values from -6 to 6
- value_vecs: bfloat16 [16384, 128], P(('pb', 'ka')), may hold values from -6 to 6
- outputs: bfloat16 [16384, 1024], P(('pb', 'ka')), may hold values from -6 to 6
- out_grad: bfloat16 [16384, 1024], P(('pb', 'ka')), may hold values from -6 to 6
- positions: int32 [16384], replicated, may hold values from 0 to 16383, as said below
Outputs:
- query_grad: bfloat16 [16384, 1024], P(('pb', 'ka'))
- key_grad: bfloat16 [16384, 128], P(('pb', 'ka'))
- value_grad: bfloat16 [16384, 128], P(('pb', 'ka'))
Inputs may be any that keep to these rules, and one draw needn't show every extreme that they name: Each aligned run of 128 rows holds 128 consecutive positions in increasing order, and the runs together hold every position of the trace once.
All inputs are finite; a program needn't handle non-finite values.
Results may differ from a plain program's by a relative error of at most 0.0051.
Values may be sent and summed in bfloat16 or wider, within the bound.
A program may use at most 64 MiB of HBM per device.

v0:
```python
import jax
import jax.numpy as jnp
from jax import lax
from jax.sharding import PartitionSpec as P

HEADS = 8
HD = 128


NEG_BIG = -1e30


def joined(value, axis, join):
    pieces = jax.tree.map(lambda part: lax.all_gather(part, axis), value)
    head = jax.tree.map(lambda part: part[0], pieces)
    tail = jax.tree.map(lambda part: part[1:], pieces)
    subtotal, _ = lax.scan(lambda subtotal, section: (join(subtotal, section), None), head, tail)
    return subtotal


def row_products(left, right):
    count = left.shape[0]
    left3 = left.reshape(count, HEADS, HD)
    right3 = right.reshape(count, HEADS, HD)
    return jnp.einsum("ahd,ahd->ha", left3, right3, preferred_element_type=jnp.float32)


def combine_stats(first, second):
    joint = jnp.maximum(first[0], second[0])
    total = first[1] * jnp.exp(first[0] - joint) + second[1] * jnp.exp(second[0] - joint)
    return (joint, total)


def tile_terms(query_t, grad_t, qpos_t, norm_t, delta_t, key_t, value_t, kpos_t):
    f32 = jnp.float32
    scaling = HD ** (-0.5)
    raw = jnp.einsum("ahd,bd->hab", query_t, key_t, preferred_element_type=f32) * scaling
    visible = kpos_t[None, None, :] <= qpos_t[None, :, None]
    masked = jnp.where(visible, raw, NEG_BIG)
    probs = jnp.where(visible, jnp.exp(masked - norm_t[:, :, None]), 0.0)
    probs_half = probs.astype(jnp.bfloat16)
    dprob = jnp.einsum("ahd,bd->hab", grad_t, value_t, preferred_element_type=f32)
    dscore = (probs * (dprob - delta_t[:, :, None])).astype(jnp.bfloat16)
    key_part = jnp.einsum("hab,ahd->bd", dscore, query_t, preferred_element_type=f32)
    value_part = jnp.einsum("hab,ahd->bd", probs_half, grad_t, preferred_element_type=f32)
    query_part = jnp.einsum("hab,bd->ahd", dscore, key_t, preferred_element_type=f32)
    return (query_part, key_part, value_part)


def local(queries, key_vecs, value_vecs, outputs, out_grad, positions):
    f32 = jnp.float32
    n_query = lax.axis_size("pb")
    n_key = lax.axis_size("ka")
    shard_rows = queries.shape[0]
    query_count = shard_rows * n_key
    key_count = shard_rows * n_query
    scaling = HD ** (-0.5)
    query_all, grad_all = (
        lax.all_gather(queries, "ka", axis=0, tiled=True),
        lax.all_gather(out_grad, "ka", axis=0, tiled=True),
    )
    output_all = lax.all_gather(outputs, "ka", axis=0, tiled=True)
    delta = row_products(grad_all, output_all)
    key_all, value_all = (
        lax.all_gather(key_vecs, "pb", axis=0, tiled=True),
        lax.all_gather(value_vecs, "pb", axis=0, tiled=True),
    )
    layout = positions.reshape(n_query, n_key, shard_rows)
    query_pos = lax.dynamic_index_in_dim(layout, lax.axis_index("pb"), 0, keepdims=False).reshape(
        query_count
    )
    key_pos = lax.dynamic_index_in_dim(layout, lax.axis_index("ka"), 1, keepdims=False).reshape(
        key_count
    )
    query3 = query_all.reshape(query_count, HEADS, HD)
    grad3 = grad_all.reshape(query_count, HEADS, HD)
    width = min(256, key_count)
    blocks = key_count // width
    key_blocks = key_all.reshape(blocks, width, HD)
    value_blocks = value_all.reshape(blocks, width, HD)
    pos_blocks = key_pos.reshape(blocks, width)

    def stats_step(carry, block):
        run_max, run_sum = carry
        raw = jnp.einsum("ahd,bd->hab", query3, block[0], preferred_element_type=f32) * scaling
        visible = block[1][None, None, :] <= query_pos[None, :, None]
        masked = jnp.where(visible, raw, NEG_BIG)
        new_max = jnp.maximum(run_max, jnp.max(masked, axis=2))
        terms = jnp.where(visible, jnp.exp(masked - new_max[:, :, None]), 0.0)
        new_sum = run_sum * jnp.exp(run_max - new_max) + jnp.sum(terms, axis=2)
        return ((new_max, new_sum), None)

    start = (jnp.full((HEADS, query_count), NEG_BIG, f32), jnp.zeros((HEADS, query_count), f32))
    (local_max, local_sum), unused = lax.scan(stats_step, start, (key_blocks, pos_blocks))
    row_max, row_sum = joined((local_max, local_sum), "ka", combine_stats)
    log_norm = row_max + jnp.log(row_sum)
    query_start = jnp.zeros((query_count, HEADS, HD), f32)

    def grad_step(query_acc, block):
        key_block, value_block, pos_block = block
        terms = tile_terms(
            query3, grad3, query_pos, log_norm, delta, key_block, value_block, pos_block
        )
        return (query_acc + terms[0], (terms[1], terms[2]))

    query_acc, parts = lax.scan(grad_step, query_start, (key_blocks, value_blocks, pos_blocks))
    key_parts, value_parts = parts
    key_sum, value_sum = (
        lax.psum_scatter(key_parts.reshape(key_count, HD), "pb", scatter_dimension=0, tiled=True),
        lax.psum_scatter(value_parts.reshape(key_count, HD), "pb", scatter_dimension=0, tiled=True),
    )
    query_sum = lax.psum_scatter(
        query_acc.reshape(query_count, HEADS * HD), "ka", scatter_dimension=0, tiled=True
    )
    return (
        (query_sum * scaling).astype(jnp.bfloat16),
        (key_sum * scaling).astype(jnp.bfloat16),
        value_sum.astype(jnp.bfloat16),
    )


def solution(mesh):
    return jax.shard_map(
        local,
        mesh=mesh,
        in_specs=(
            P(("pb", "ka"), None),
            P(("pb", "ka"), None),
            P(("pb", "ka"), None),
            P(("pb", "ka"), None),
            P(("pb", "ka"), None),
            P(),
        ),
        out_specs=(P(("pb", "ka"), None), P(("pb", "ka"), None), P(("pb", "ka"), None)),
        check_vma=False,
    )
```

profile of v0, /device:TPU:1, one launch (start us, length us, event | category | flops | bytes accessed | tf_op | source)
XLA Modules:
  0.0 498.1 jit_solution(14912517835885570102)
XLA Ops:
  10.7 42.4 %all_gather.27 = bf16[1024,128]{1,0:T(8,128)(2,1)S(1)} all-gather(bf16[64,128]{1,0:T(8,128)(2,1)} %param.13), channel_id=1, replica_groups=mesh['pb'=16,'ka'=16] {'pb'}, dimensions={0}, use_global_device_ids=true | all-gather | bytes 278528 | tf_op jit(solution)/shard_map/all_gather | solution.py:65
  53.1 35.6 %all_gather.33 = bf16[1024,128]{1,0:T(8,128)(2,1)} all-gather(bf16[64,128]{1,0:T(8,128)(2,1)} %param.14), channel_id=1, replica_groups=mesh['pb'=16,'ka'=16] {'pb'}, dimensions={0}, use_global_device_ids=true | all-gather | bytes 278528 | tf_op jit(solution)/shard_map/all_gather | solution.py:66
  88.7 4.0 copy.22
  95.7 15.7 %while.43 = (s32[]{:T(128)}, f32[8,1024]{1,0:T(8,128)S(1)}, f32[8,1024]{1,0:T(8,128)S(1)}, s32[4,256]{1,0:T(4,128)S(1)}, s32[16,64]{1,0:T(8,128)}, /*index=5*/bf...) while((s32[]{:T(128)}, f32[8,1024]{1,0:T(8,128)S(1)}, ...), condition=%wide.wide.region_3.4_spmd.clone, body=%wide.wide.region_0.3_spmd.clone.sunk | while | flops 553951232 | bytes 20159616 | solution.py:94
  111.5 34.9 %all-gather.1 = f32[128,1024]{1,0:T(8,128)S(1)} all-gather(f32[8,1024]{1,0:T(8,128)S(1)} %get-tuple-element.134), channel_id=3, replica_groups=mesh['pb'=16,'ka'=16] {'ka'}, dimensions={0}, use_global_device_ids=true | all-gather | bytes 557056 | tf_op jit(solution)/shard_map/all_gather | solution.py:14
  146.4 17.9 %all-gather = f32[128,1024]{1,0:T(8,128)S(1)} all-gather(f32[8,1024]{1,0:T(8,128)S(1)} %get-tuple-element.133), channel_id=2, replica_groups=mesh['pb'=16,'ka'=16] {'ka'}, dimensions={0}, use_global_device_ids=true | all-gather | bytes 557056 | tf_op jit(solution)/shard_map/all_gather | solution.py:14
  164.2 3.6 copy.40
  168.7 12.2 %while.42 = (s32[]{:T(128)}, f32[8,1024]{1,0:T(8,128)S(1)}, f32[8,1024]{1,0:T(8,128)S(1)}, f32[15,8,1024]{2,1,0:T(8,128)S(1)}, f32[15,8,1024]{2,1,0:T(8,128)}, /*index=5*/s32[]{:T(128)}) while((s32[]{:T(128)}, f32[8,1024]{1,0:T(8,128)S(1)}, f32[8,1024]{1,0:T(8,128)S(1)}, f32[15,8,1024]{2,1,0:T(8,128)S(1)}, f32[15,8,1024]{2,1,0:T(8,128)}, ...), condition=%wide.region_5.6_spmd, body=%wide.region_4.5_spmd.sunk | while | flops 49154 | bytes 196689 | solution.py:17
  180.9 3.9 copy.24
  184.8 3.9 copy.26
  188.7 4.3 copy.35
  193.1 4.1 multiply_reduce_fusion
  197.3 58.9 %while.44 = (s32[]{:T(128)}, f32[1024,8,128]{0,2,1:T(8,128)}, f32[4,256,128]{2,1,0:T(8,128)}, f32[4,256,128]{2,1,0:T(8,128)}, bf16[4,256,128]{2,1,0:T(8,128)(2,1...) while((s32[]{:T(128)}, f32[1024,8,128]{0,2,1:T(8,128)}, ...), condition=%wide.wide.region_7.8_spmd.clone, body=%wide.wide.region_6.7_spmd.clone.sunk | while | flops 2711879680 | bytes 97819904 | solution.py:106
  199.2 3.1 fusion.96
  202.3 4.0 fusion.94
  217.0 4.0 fusion.94
  228.6 3.1 fusion.96
  231.7 4.0 fusion.94
  243.3 3.2 fusion.96
  246.4 4.0 fusion.94
  256.8 5.4 %copy.38 = f32[1024,1024]{1,0:T(8,128)} copy(f32[1024,1024]{0,1:T(8,128)} %bitcast.165) | data formatting | bytes 8388608 | tf_op jit(solution)/shard_map/reshape | solution.py:113
  262.3 72.5 %reduce-scatter.8.cloned.1.call-done = f32[64,128]{1,0:T(8,128)} async-done(((f32[1024,128]{1,0:T(8,128)}), f32[64,128]{1,0:T(8,128)}) %reduce-scatter.8.cloned.1.call-update) | async-done | bytes 32784 | tf_op jit(solution)/shard_map/reduce_scatter | solution.py:110
  336.2 85.7 %reduce-scatter.6.cloned.1.call-done = f32[64,128]{1,0:T(8,128)} async-done(((f32[1024,128]{1,0:T(8,128)}), f32[64,128]{1,0:T(8,128)}) %reduce-scatter.6.cloned.1.call-update) | async-done | bytes 32784 | tf_op jit(solution)/shard_map/reduce_scatter | solution.py:109
  423.2 66.3 %reduce-scatter.4.cloned.1.call-done = f32[64,1024]{1,0:T(8,128)} async-done(((f32[1024,1024]{1,0:T(8,128)}), f32[64,1024]{1,0:T(8,128)}) %reduce-scatter.4.cloned.1.call-update) | async-done | bytes 262160 | tf_op jit(solution)/shard_map/reduce_scatter | solution.py:112
  (126 shorter events, 73.2 us)
Async XLA Ops:
  7.2 81.6 %all-gather.6.cloned.1.call-start = ((), (), s32[]{:S(2)}) async-start(), calls=%async_computation.3 | async-start | bytes 2228224 | tf_op jit(solution)/shard_map/all_gather | solution.py:59
  7.9 156.3 %all-gather.10.cloned.1.call-start = ((), (), s32[]{:S(2)}) async-start(), calls=%async_computation.5 | async-start | bytes 2228224 | tf_op jit(solution)/shard_map/all_gather | solution.py:62
  8.6 172.2 %all-gather.8.cloned.1.call-start = ((), (), s32[]{:S(2)}) async-start(), calls=%async_computation.4 | async-start | bytes 2228224 | tf_op jit(solution)/shard_map/all_gather | solution.py:60
  9.4 325.4 %reduce-scatter.8.cloned.1.call-start = ((), (), s32[]{:S(2)}) async-start(), calls=%async_computation.8 | async-start | bytes 557056 | tf_op jit(solution)/shard_map/reduce_scatter | solution.py:110
  10.4 85.3 %copy-start.3 = (s32[16,64]{1,0:T(8,128)}, s32[16,64]{1,0:T(8,128)S(1)}, u32[]{:S(2)}) copy-start(s32[16,64]{1,0:T(8,128)S(1)} %dynamic-slice_bitcast_fusion) | copy-start | bytes 12292
  197.6 1.6 copy-start.2
  206.3 2.2 copy-start
  210.1 1.9 copy-start.1
  212.3 1.6 copy-start.2
  221.0 2.2 copy-start
  224.8 1.9 copy-start.1
  227.0 1.6 copy-start.2
  235.7 2.2 copy-start
  239.5 1.9 copy-start.1
  241.7 1.6 copy-start.2
  250.4 2.2 copy-start
  254.2 1.9 copy-start.1
  256.2 165.7 %reduce-scatter.6.cloned.1.call-start = ((), (), s32[]{:S(2)}) async-start(), calls=%async_computation.7 | async-start | bytes 557056 | tf_op jit(solution)/shard_map/reduce_scatter | solution.py:109
  256.8 232.8 %reduce-scatter.4.cloned.1.call-start = ((), (), s32[]{:S(2)}) async-start(), calls=%async_computation.6 | async-start | bytes 4456448 | tf_op jit(solution)/shard_map/reduce_scatter | solution.py:112
Sparse Core Ops, SparseCore 0:
  9.8 40.9 all-gather.5
  52.7 36.9 all-gather.9
  91.5 37.0 all-gather.7
  256.3 78.4 reduce-scatter.7
  338.5 83.3 reduce-scatter.5
  424.3 65.2 reduce-scatter.3
where the time goes:
time: 503 us; the launch traced here: 498 us
  waiting for transfers between devices  227 us (45%)
  blocking collectives  131 us (26%)
  matrix products  53.8 us (11%)
  local copies, waits for them, and re-layouts  40.5 us (8%)
  other arithmetic  30.5 us (6%)
  between operations  14.2 us (3%)
    reduce_scatter x1, waiting for transfers between devices, local(): lax.psum_scatter(key_parts.reshape(key_count, HD), 'pb', scatter_dimensio...  85.7 us
    reduce_scatter x1, waiting for transfers between devices, local(): lax.psum_scatter(value_parts.reshape(key_count, HD), 'pb', scatter_dimens...  72.5 us
    reduce_scatter x1, waiting for transfers between devices, local(): lax.psum_scatter(query_acc.reshape(query_count, HEADS * HD), 'ka', scatte...  66.3 us
    all_gather x2, blocking collectives, joined(): pieces = jax.tree.map(lambda part: lax.all_gather(part, axis), value)  52.7 us
    all_gather x1, blocking collectives, local(): lax.all_gather(key_vecs, 'pb', axis=0, tiled=True)  42.4 us
    all_gather x1, blocking collectives, local(): lax.all_gather(value_vecs, 'pb', axis=0, tiled=True)  35.6 us
    dot_general x4, matrix products, tile_terms(): jnp.einsum('ahd,bd->hab', grad_t, value_t, preferred_element_type=f32)  15.9 us
    unnamed x6, local copies, waits for them, and re-layouts  14.8 us
  transfers between devices with their start and end apart: 6, of which 3 were waited for; matrix products, arithmetic and copies ran while one was open for 10% of the time, Pallas kernels for 0%

commit v1 on v0

v1 whole, which is shorter than its diff:
```python
import math

import jax
import jax.numpy as jnp
from jax import lax
from jax.experimental import pallas as pl
from jax.experimental.pallas import tpu as pltpu
from jax.sharding import PartitionSpec as P

HEADS = 8
HD = 128
NX, NY, NZ, NC = 4, 4, 8, 2
ROWS = 64
WIDE = HEADS * ROWS
COLS = NX * WIDE
TILE = NC * NY * ROWS
HALF = NY * ROWS

HIDDEN = -1e30
FLOOR = -1e20
SCALE = HD ** -0.5
LOG2E = math.log2(math.e)

f32 = jnp.float32
bf16 = jnp.bfloat16
MESH = pl.DeviceIdType.MESH


def dot(left, right, cl, cr):
    return lax.dot_general(
        left, right, (((cl,), (cr,)), ((), ())), preferred_element_type=f32
    )


def where_is(x, y, z, c):
    return {"pb": y * 4 + z // 2, "ka": (z % 2) * 8 + x * 2 + c}


def shard_of(x, y, z, c):
    return (y * 4 + z // 2) * 16 + (z % 2) * 8 + x * 2 + c


def offset_of(j):
    return ((j + 1) // 2) * (2 * (j % 2) - 1)


def kernel(
    starts, q_in, k_in, v_in, o_in, d_in,
    dq_out, dk_out, dv_out,
    q_all, d_all, delta, lse_own, lse_got, lse,
    k_all, v_all, k_pos, q_pos,
    s_even, s_odd, top, total,
    dq_acc, dq_send, dq_got, stage,
    own, core_send, core_got, y_send, y_got, z_send, z_got,
    qs, qr, ds, dr, es, er, ls, lr, gs, gr,
    kzs, kzr, kys, kyr, kcs, kcr,
    vzs, vzr, vys, vyr, vcs, vcr,
    pcs, pcr, pys, pyr, pzs, pzr,
):
    pb, ka = lax.axis_index("pb"), lax.axis_index("ka")
    y = pb // 4
    z = (pb % 4) * 2 + ka // 8
    x = (ka // 2) % 4
    c = ka % 2

    def send(src, dst, ssem, rsem, to):
        return pltpu.make_async_remote_copy(
            src_ref=src, dst_ref=dst, send_sem=ssem, recv_sem=rsem,
            device_id=to, device_id_type=MESH,
        )

    core_peer = where_is(x, y, z, 1 - c)

    def x_peer(e):
        return where_is((x + e) % NX, y, z, c)

    def y_peer(e):
        return where_is(x, (y + e) % NY, z, c)

    def z_peer(e):
        return where_is(x, y, (z + e) % NZ, c)

    barrier = pltpu.get_barrier_semaphore()
    peers = [core_peer]
    peers += [x_peer(e) for e in range(1, NX)]
    peers += [y_peer(e) for e in range(1, NY)]
    peers += [z_peer(e) for e in range(1, NZ)]
    for peer in peers:
        pl.semaphore_signal(barrier, inc=1, device_id=peer, device_id_type=MESH)

    q = q_in[...]
    d = d_in[...]
    for h in range(HEADS):
        rows = pl.ds(h * ROWS, ROWS)
        q_all[x, rows, :] = q[:, h * HD:(h + 1) * HD]
        d_all[x, rows, :] = d[:, h * HD:(h + 1) * HD]
    k_all[z, c, y] = k_in[...]
    v_all[z, c, y] = v_in[...]

    pl.semaphore_wait(barrier, len(peers))

    def q_copy(e):
        return send(q_all.at[x], q_all.at[x], qs.at[e - 1], qr.at[e - 1], x_peer(e))

    def d_copy(e):
        return send(d_all.at[x], d_all.at[x], ds.at[e - 1], dr.at[e - 1], x_peer(e))

    def e_copy(e):
        return send(delta.at[x], delta.at[x], es.at[e - 1], er.at[e - 1], x_peer(e))

    def l_copy(e):
        return send(lse_own, lse_got.at[e - 1], ls.at[e - 1], lr.at[e - 1], x_peer(e))

    def g_copy(e):
        return send(dq_send.at[e - 1], dq_got.at[e - 1], gs.at[e - 1], gr.at[e - 1], x_peer(e))

    def kz_copy(e):
        own_k = k_all.at[z, c, y]
        return send(own_k, own_k, kzs.at[e - 1], kzr.at[e - 1], z_peer(e))

    def vz_copy(e):
        own_v = v_all.at[z, c, y]
        return send(own_v, own_v, vzs.at[e - 1], vzr.at[e - 1], z_peer(e))

    def ky_copy(j, e):
        part = k_all.at[(z + offset_of(j) + NZ) % NZ, c, y]
        return send(part, part, kys.at[j, e - 1], kyr.at[j, e - 1], y_peer(e))

    def vy_copy(j, e):
        part = v_all.at[(z + offset_of(j) + NZ) % NZ, c, y]
        return send(part, part, vys.at[j, e - 1], vyr.at[j, e - 1], y_peer(e))

    def kc_copy(j):
        part = k_all.at[(z + offset_of(j) + NZ) % NZ, c]
        return send(part, part, kcs.at[j], kcr.at[j], core_peer)

    def vc_copy(j):
        part = v_all.at[(z + offset_of(j) + NZ) % NZ, c]
        return send(part, part, vcs.at[j], vcr.at[j], core_peer)

    for e in range(1, NX):
        q_copy(e).start()
    for e in (1, 7, 2, 6, 3, 5, 4):
        kz_copy(e).start()
    for e in range(1, NY):
        ky_copy(0, e).start()
    for e in (1, 7, 2, 6, 3, 5, 4):
        vz_copy(e).start()
    for e in range(1, NY):
        vy_copy(0, e).start()

    o = o_in[...].astype(f32) * d.astype(f32)
    prod = jnp.concatenate([o[:, h * HD:(h + 1) * HD] for h in range(HEADS)], axis=0)
    high = prod.astype(bf16)
    low = (prod - high.astype(f32)).astype(bf16)
    ones = jnp.ones((8, HD), bf16)
    delta[x] = dot(ones, high, 1, 1) + dot(ones, low, 1, 1)

    row = lax.broadcasted_iota(jnp.int32, (ROWS, HD), 0)
    lane = lax.broadcasted_iota(jnp.int32, (8, WIDE), 1) % ROWS

    def place_keys(n, _):
        j, cc, yy = n // (NC * NY), (n // NY) % NC, n % NY
        zz = (z + offset_of(j) + NZ) % NZ
        at = pl.ds(pl.multiple_of(n * ROWS, ROWS), ROWS)
        k_pos[at, :] = row + starts[shard_of(x, yy, zz, cc)]
        return 0

    lax.fori_loop(0, NZ * NC * NY, place_keys, 0)
    for xx in range(NX):
        q_pos[:, xx * WIDE:(xx + 1) * WIDE] = lane + starts[shard_of(xx, y, z, c)]

    top[...] = jnp.full_like(top, FLOOR)
    total[...] = jnp.zeros_like(total)
    dq_acc[...] = jnp.zeros_like(dq_acc)

    def forward_keys(j, _):
        arrived = (NZ - offset_of(j)) % NZ
        kz_copy(arrived).wait_recv()
        for e in range(1, NY):
            ky_copy(j, e).start()
        return 0

    lax.fori_loop(1, NZ, forward_keys, 0)

    def share_keys(j):
        for e in range(1, NY):
            ky_copy(j, e).wait_recv()
        kc_copy(j).start()

    share_keys(0)
    for e in range(1, NX):
        q_copy(e).wait_recv()
    for e in range(1, NX):
        d_copy(e).start()
        e_copy(e).start()

    def arrive(j):
        @pl.when(j < NZ - 1)
        def _():
            share_keys(j + 1)
            vz_copy((NZ - offset_of(j + 1)) % NZ).wait_recv()
            for e in range(1, NY):
                vy_copy(j + 1, e).start()

        kc_copy(j).wait_recv()

    def scores(j, store, t):
        zz = (z + offset_of(j) + NZ) % NZ
        keys = k_all[zz].reshape(TILE, HD)
        queries = q_all[...].reshape(COLS, HD)
        raw = dot(keys, queries, 1, 1) * (SCALE * LOG2E)
        at = pl.ds(pl.multiple_of(j * TILE, TILE), TILE)
        spot = jnp.concatenate([k_pos[at, :]] * (COLS // HD), axis=1)
        raw = jnp.where(spot <= q_pos[0:1, :], raw, HIDDEN)
        store[t] = raw
        return jnp.max(raw.reshape(TILE // 8, 8, COLS), axis=0)

    def sums(store, t, high):
        part = store[t].reshape(TILE // 8, 8, COLS)
        return jnp.sum(jnp.exp2(part - high[None]), axis=0)

    arrive(0)
    top[...] = jnp.maximum(top[...], scores(0, s_even, 0))

    def pair(t, _):
        high = top[...]
        arrive(2 * t + 1)
        seen = scores(2 * t + 1, s_odd, t)
        run = total[...] + sums(s_even, t, high)
        new = jnp.maximum(high, seen)
        total[...] = run * jnp.exp2(high - new)
        top[...] = new

        @pl.when(t < NZ // 2 - 1)
        def _():
            high = top[...]
            arrive(2 * t + 2)
            seen = scores(2 * t + 2, s_even, t + 1)
            run = total[...] + sums(s_odd, t, high)
            new = jnp.maximum(high, seen)
            total[...] = run * jnp.exp2(high - new)
            top[...] = new

        return 0

    lax.fori_loop(0, NZ // 2, pair, 0)
    high = top[...]
    run = total[...] + sums(s_odd, NZ // 2 - 1, high)
    peak = jnp.max(high, axis=0, keepdims=True)
    mass = jnp.sum(run * jnp.exp2(high - peak), axis=0, keepdims=True)
    mine = jnp.where(mass > 0.0, peak + jnp.log2(mass), FLOOR)
    for n in range(8):
        lse_own[n:n + 1, :] = mine[:, n * 256:(n + 1) * 256]
    for e in range(1, NX):
        l_copy(e).start()

    def share_values(j, _):
        for e in range(1, NY):
            vy_copy(j, e).wait_recv()
        vc_copy(j).start()
        return 0

    lax.fori_loop(0, NZ, share_values, 0)

    for e in range(1, NX):
        l_copy(e).wait_recv()
    parts = [lse_own[...]] + [lse_got[e] for e in range(NX - 1)]
    peak = jnp.maximum(jnp.maximum(parts[0], parts[1]), jnp.maximum(parts[2], parts[3]))
    mass = sum(jnp.exp2(part - peak) for part in parts)
    joint = peak + jnp.log2(mass)
    for n in range(8):
        lse[:, n * 256:(n + 1) * 256] = joint[n:n + 1, :]
    for e in range(1, NX):
        d_copy(e).wait_recv()
        e_copy(e).wait_recv()

    def pc_copy(i):
        return send(core_send.at[i], core_got.at[i], pcs.at[i], pcr.at[i], core_peer)

    def py_copy(i, e):
        return send(
            y_send.at[i, (y + e) % NY], y_got.at[i, e - 1],
            pys.at[i, e - 1], pyr.at[i, e - 1], y_peer(e),
        )

    def pz_copy(i, e):
        return send(z_send.at[i], z_got.at[e - 1], pzs.at[e - 1], pzr.at[e - 1], z_peer(e))

    def fold_core(i):
        pc_copy(i).wait_recv()
        both = own[i] + core_got[i].astype(f32)
        y_send[i] = both.astype(bf16).reshape(NY, ROWS, 2 * HD)
        for e in range(1, NY):
            py_copy(i, e).start()

    def fold_y(i):
        for e in range(1, NY):
            py_copy(i, e).wait_recv()
        part = y_send[i, y].astype(f32)
        for e in range(NY - 1):
            part = part + y_got[i, e].astype(f32)
        return part

    def send_z(i):
        z_send[i] = fold_y(i).astype(bf16)
        pz_copy(i, (offset_of(NZ - 1 - i) + NZ) % NZ).start()

    delta_row = jnp.concatenate([delta[xx, 0:1, :] for xx in range(NX)], axis=1)

    def grad(i, store, t):
        j = NZ - 1 - i
        zz = (z + offset_of(j) + NZ) % NZ

        @pl.when(i >= 1)
        def _():
            fold_core(i - 1)

        @pl.when(i >= 2)
        def _():
            send_z(i - 2)

        vc_copy(j).wait_recv()
        keys = k_all[zz].reshape(TILE, HD)
        values = v_all[zz].reshape(TILE, HD)
        queries = q_all[...].reshape(COLS, HD)
        cots = d_all[...].reshape(COLS, HD)
        dprob = dot(values, cots, 1, 1)
        probs = jnp.exp2(store[t] - lse[...])
        dscore = (probs * (dprob - delta_row)).astype(bf16)
        half = probs.astype(bf16)
        dq_acc[...] += dot(keys, dscore, 0, 0)
        own_rows = pl.ds(pl.multiple_of(c * HALF, HALF), HALF)
        gone_rows = pl.ds(pl.multiple_of((1 - c) * HALF, HALF), HALF)
        stage[:, 0:HD] = dot(dscore, queries, 1, 0) * SCALE
        stage[:, HD:2 * HD] = dot(half, cots, 1, 0)
        core_send[i] = stage[gone_rows, :].astype(bf16)
        pc_copy(i).start()
        own[i] = stage[own_rows, :]

    def grad_pair(t, _):
        grad(2 * t, s_odd, NZ // 2 - 1 - t)
        grad(2 * t + 1, s_even, NZ // 2 - 1 - t)
        return 0

    lax.fori_loop(0, NZ // 2, grad_pair, 0)

    for e in range(1, NX):
        cols = pl.ds(pl.multiple_of(((x + e) % NX) * WIDE, WIDE), WIDE)
        dq_send[e - 1] = dq_acc[:, cols].astype(bf16)
        g_copy(e).start()
    fold_core(NZ - 1)
    send_z(NZ - 2)
    kv_sum = fold_y(NZ - 1)

    mine = pl.ds(pl.multiple_of(x * WIDE, WIDE), WIDE)
    dq_sum = dq_acc[:, mine]
    for e in range(1, NX):
        g_copy(e).wait_recv()
        dq_sum = dq_sum + dq_got[e - 1].astype(f32)
    dq_rows = jnp.transpose(dq_sum * SCALE).astype(bf16)
    for h in range(HEADS):
        dq_out[:, h * HD:(h + 1) * HD] = dq_rows[h * ROWS:(h + 1) * ROWS, :]

    for e in range(1, NZ):
        pz_copy(0, e).wait_recv()
        kv_sum = kv_sum + z_got[e - 1].astype(f32)
    dk_out[...] = kv_sum[:, 0:HD].astype(bf16)
    dv_out[...] = kv_sum[:, HD:2 * HD].astype(bf16)

    for e in range(1, NX):
        q_copy(e).wait_send()
        d_copy(e).wait_send()
        e_copy(e).wait_send()
        l_copy(e).wait_send()
        g_copy(e).wait_send()
    for e in range(1, NZ):
        kz_copy(e).wait_send()
        vz_copy(e).wait_send()
        pz_copy(0, e).wait_send()

    def drain(j, _):
        for e in range(1, NY):
            ky_copy(j, e).wait_send()
            vy_copy(j, e).wait_send()
            py_copy(j, e).wait_send()
        kc_copy(j).wait_send()
        vc_copy(j).wait_send()
        pc_copy(j).wait_send()
        return 0

    lax.fori_loop(0, NZ, drain, 0)


def local(queries, key_vecs, value_vecs, outputs, out_grad, positions):
    starts = positions[::ROWS]
    vmem = pl.BlockSpec(memory_space=pltpu.VMEM)
    dma = pltpu.SemaphoreType.DMA
    V = pltpu.VMEM
    return pl.pallas_call(
        kernel,
        out_shape=(
            jax.ShapeDtypeStruct((ROWS, HEADS * HD), bf16),
            jax.ShapeDtypeStruct((ROWS, HD), bf16),
            jax.ShapeDtypeStruct((ROWS, HD), bf16),
        ),
        in_specs=[pl.BlockSpec(memory_space=pltpu.SMEM)] + [vmem] * 5,
        out_specs=(vmem, vmem, vmem),
        scratch_shapes=[
            V((NX, WIDE, HD), bf16), V((NX, WIDE, HD), bf16),
            V((NX, 8, WIDE), f32),
            V((8, 256), f32), V((NX - 1, 8, 256), f32), V((1, COLS), f32),
            V((NZ, NC, NY, ROWS, HD), bf16), V((NZ, NC, NY, ROWS, HD), bf16),
            V((NZ * TILE, HD), jnp.int32), V((8, COLS), jnp.int32),
            V((NZ // 2, TILE, COLS), f32), V((NZ // 2, TILE, COLS), f32),
            V((8, COLS), f32), V((8, COLS), f32),
            V((HD, COLS), f32), V((NX - 1, HD, WIDE), bf16), V((NX - 1, HD, WIDE), bf16),
            V((TILE, 2 * HD), f32),
            V((NZ, HALF, 2 * HD), f32),
            V((NZ, HALF, 2 * HD), bf16), V((NZ, HALF, 2 * HD), bf16),
            V((NZ, NY, ROWS, 2 * HD), bf16), V((NZ, NY - 1, ROWS, 2 * HD), bf16),
            V((NZ, ROWS, 2 * HD), bf16), V((NZ - 1, ROWS, 2 * HD), bf16),
        ]
        + [dma((NX - 1,))] * 10
        + [dma((NZ - 1,)), dma((NZ - 1,)), dma((NZ, NY - 1)), dma((NZ, NY - 1)), dma((NZ,)), dma((NZ,))] * 2
        + [dma((NZ,)), dma((NZ,)), dma((NZ, NY - 1)), dma((NZ, NY - 1)), dma((NZ - 1,)), dma((NZ - 1,))],
        compiler_params=pltpu.CompilerParams(
            collective_id=0, has_side_effects=True, vmem_limit_bytes=62 * 2**20
        ),
        cost_estimate=pl.CostEstimate(
            flops=12 * COLS * NZ * TILE * HD, bytes_accessed=1 << 20, transcendentals=2 * COLS * NZ * TILE
        ),
    )(starts, queries, key_vecs, value_vecs, outputs, out_grad)


def solution(mesh):
    rows = P(("pb", "ka"), None)
    return jax.shard_map(
        local,
        mesh=mesh,
        in_specs=(rows, rows, rows, rows, rows, P()),
        out_specs=(rows, rows, rows),
        check_vma=False,
    )
```

time: 503 us -> 83.3 us (0.17)
  waiting for transfers between devices: 227 us -> 0 us
  blocking collectives: 131 us -> 0 us
  Pallas kernels: 0 us -> 77.9 us
  matrix products: 53.8 us -> 0 us
  local copies, waits for them, and re-layouts: 40.5 us -> 4.52 us
  other arithmetic: 30.5 us -> 0 us
  between operations: 14.2 us -> 0.65 us
    reduce_scatter x3 -> x0, waiting for transfers between devices: 225 us -> none  [the longest x1 85.7 us: local(): lax.psum_scatter(key_parts.reshape(key_count, HD), 'pb', scatter_dimensio...]
    all_gather x4 -> x0, blocking collectives: 131 us -> none  [the longest x2 52.7 us: joined(): pieces = jax.tree.map(lambda part: lax.all_gather(part, axis), value)]
    pallas_call x0 -> x1, Pallas kernels: none -> 77.9 us  [local(): pl.pallas_call(kernel, out_shape=(jax.ShapeDtypeStruct((ROWS, HEADS * HD)...]
    dot_general x24 -> x0, matrix products: 53.8 us -> none  [the longest x4 15.9 us: tile_terms(): jnp.einsum('ahd,bd->hab', grad_t, value_t, preferred_element_type=f32)]
    add x20 -> x0, other arithmetic: 12.1 us -> none  [the longest x15 12 us: combine_stats(): first[1] * jnp.exp(first[0] - joint)]
    unnamed x6 -> x7, local copies, waits for them, and re-layouts: 14.8 us -> 2.91 us
    while x28 -> x0, local copies, waits for them, and re-layouts: 10.2 us -> none
    reduce_sum x4 -> x0, other arithmetic: 8.26 us -> none  [stats_step(): new_sum = run_sum * jnp.exp(run_max - new_max) + jnp.sum(terms, axis=2)]
  transfers between devices with their start and end apart: 6 -> 0, of which waited for: 3 -> 0; matrix products, arithmetic and copies ran while one was open for 10% -> 0% of each run, Pallas kernels for 0% -> 0%
where the time goes in v1:
time: 83.3 us; the launch traced here: 83.1 us
  Pallas kernels  77.9 us (94%)
  local copies, waits for them, and re-layouts  4.52 us (5%)
    pallas_call x1, Pallas kernels, local(): pl.pallas_call(kernel, out_shape=(jax.ShapeDtypeStruct((ROWS, HEADS * HD)...  77.9 us
    unnamed x7, local copies, waits for them, and re-layouts  2.91 us

profile of v1, /device:TPU:1, one launch (start us, length us, event | category | flops | bytes accessed | tf_op | source)
XLA Modules:
  0.0 83.1 jit_solution(6006776817215526026)
XLA Ops:
  0.6 1.6 %slice.3.starts = s32[256]{0:T(256)} slice(s32[16384]{0:T(1024)} %param.11), slice={[0:16384:64]} | slice | bytes 2048 | tf_op jit(solution)/shard_map/slice | solution.py:396
  2.2 77.9 %shard_map.85 = (bf16[64,1024]{1,0:T(8,128)(2,1)}, bf16[64,128]{1,0:T(8,128)(2,1)}, bf16[64,128]{1,0:T(8,128)(2,1)}) custom-call(s32[256]{0:T(256)} %slice.3.starts, bf16[64,1024]{1,0:T(8,128)(2,1)} %q_in.1, bf16[64,128]{1,0:T(8,128)(2,1)} %k_in.1, bf16[64,128]{1,0:T(8,128)(2,1)} %v_in.1, bf16[64,1024]{1,0:T(8,128)(2,1)} %o_in.1, bf16[64,1024]{1,0:T(8,128)(2,1)} %d_in.1), custom_call_target="tpu_custom_call" | custom-call | flops 12884901888 | bytes 1048576 | tf_op jit(solution)/shard_map/pallas_call | solution.py:400
  80.1 0.0 copy-start.1
  80.1 1.6 %copy.12 = bf16[64,1024]{1,0:T(8,128)(2,1)} copy(bf16[64,1024]{1,0:T(8,128)(2,1)} %get-tuple-element.6) | data formatting | bytes 262144
  81.7 0.0 copy-done.1
  81.7 0.0 copy-start
  81.7 0.6 copy.13
  82.3 0.1 copy-done
  82.5 0.6 copy.14
Async XLA Ops:
  80.1 1.6 %copy-start.1 = (bf16[64,128]{1,0:T(8,128)(2,1)S(1)}, bf16[64,128]{1,0:T(8,128)(2,1)}, u32[]{:S(2)}) copy-start(bf16[64,128]{1,0:T(8,128)(2,1)} %get-tuple-element.7) | copy-start | bytes 49156
  81.7 0.7 copy-start

commit v2 on v1

v2 whole, which is shorter than its diff:
```python
import math

import jax
import jax.numpy as jnp
from jax import lax
from jax.experimental import pallas as pl
from jax.experimental.pallas import tpu as pltpu
from jax.sharding import PartitionSpec as P

HEADS = 8
HD = 128
NX, NY, NZ, NC = 4, 4, 8, 2
ROWS = 64
WIDE = HEADS * ROWS
COLS = NX * WIDE
PART = WIDE // 2
SIDE = COLS // 2
TILE = NC * NY * ROWS
AHEAD = 3
HALF = NY * ROWS

HIDDEN = -1e30
FLOOR = -1e20
SCALE = HD ** -0.5
LOG2E = math.log2(math.e)

f32 = jnp.float32
bf16 = jnp.bfloat16
MESH = pl.DeviceIdType.MESH


def dot(left, right, cl, cr):
    return lax.dot_general(
        left, right, (((cl,), (cr,)), ((), ())), preferred_element_type=f32
    )


def where_is(x, y, z, c):
    return {"pb": y * 4 + z // 2, "ka": (z % 2) * 8 + x * 2 + c}


def offset_of(j):
    return ((j + 1) // 2) * (2 * (j % 2) - 1)


def kernel(
    p_hbm, q_hbm, k_hbm, v_hbm, o_hbm, d_hbm,
    dq_hbm, dk_hbm, dv_hbm,
    p_in, q_in, o_in, d_in, dq_out, dk_out, dv_out, ios,
    q_all, d_all, delta, lse_own, lse_got, lse,
    k_all, v_all, k_mask, q_mask,
    s_even, s_odd, top, total,
    dq_acc, dq_send, dq_got, stage, stage2,
    own, core_send, core_got, y_send, y_got, z_send, z_got,
    qs, qr, ds, dr, es, er, ls, lr, gs, gr,
    kzs, kzr, kys, kyr, kcs, kcr,
    vzs, vzr, vys, vyr, vcs, vcr,
    pcs, pcr, pys, pyr, pzs, pzr,
):
    pb, ka = lax.axis_index("pb"), lax.axis_index("ka")
    y = pb // 4
    z = (pb % 4) * 2 + ka // 8
    x = (ka // 2) % 4
    c = ka % 2

    def send(src, dst, ssem, rsem, to):
        return pltpu.make_async_remote_copy(
            src_ref=src, dst_ref=dst, send_sem=ssem, recv_sem=rsem,
            device_id=to, device_id_type=MESH,
        )

    core_peer = where_is(x, y, z, 1 - c)

    def x_peer(e):
        return where_is((x + e) % NX, y, z, c)

    def y_peer(e):
        return where_is(x, (y + e) % NY, z, c)

    def z_peer(e):
        return where_is(x, y, (z + e) % NZ, c)

    barrier = pltpu.get_barrier_semaphore()
    peers = [core_peer]
    peers += [x_peer(e) for e in range(1, NX)]
    peers += [y_peer(e) for e in range(1, NY)]
    peers += [z_peer(e) for e in range(1, NZ)]
    for peer in peers:
        pl.semaphore_signal(barrier, inc=1, device_id=peer, device_id_type=MESH)

    loads = [
        pltpu.make_async_copy(src, dst, ios.at[n])
        for n, (src, dst) in enumerate((
            (q_hbm, q_in), (k_hbm, k_all.at[z, c, y]), (d_hbm, d_in),
            (v_hbm, v_all.at[z, c, y]), (o_hbm, o_in), (p_hbm, p_in),
        ))
    ]
    for load in loads:
        load.start()
    for load in loads:
        load.wait()
    q = q_in[...]
    d = d_in[...]
    for h in range(HEADS):
        rows = pl.ds((h % 4) * ROWS, ROWS)
        q_all[h // 4, x, rows, :] = q[:, h * HD:(h + 1) * HD]
        d_all[h // 4, x, rows, :] = d[:, h * HD:(h + 1) * HD]

    pl.semaphore_wait(barrier, len(peers))

    def q_copy(side, e):
        part = q_all.at[side, x]
        return send(part, part, qs.at[side, e - 1], qr.at[side, e - 1], x_peer(e))

    def d_copy(e):
        part = d_all.at[:, x]
        return send(part, part, ds.at[e - 1], dr.at[e - 1], x_peer(e))

    def e_copy(e):
        return send(delta.at[x], delta.at[x], es.at[e - 1], er.at[e - 1], x_peer(e))

    def l_copy(side, e):
        return send(
            lse_own.at[side], lse_got.at[side, e - 1],
            ls.at[side, e - 1], lr.at[side, e - 1], x_peer(e),
        )

    def g_copy(e):
        return send(dq_send.at[e - 1], dq_got.at[e - 1], gs.at[e - 1], gr.at[e - 1], x_peer(e))

    def kz_copy(e):
        own_k = k_all.at[z, c, y]
        return send(own_k, own_k, kzs.at[e - 1], kzr.at[e - 1], z_peer(e))

    def vz_copy(e):
        own_v = v_all.at[z, c, y]
        return send(own_v, own_v, vzs.at[e - 1], vzr.at[e - 1], z_peer(e))

    def ky_copy(j, e):
        part = k_all.at[(z + offset_of(j) + NZ) % NZ, c, y]
        return send(part, part, kys.at[j, e - 1], kyr.at[j, e - 1], y_peer(e))

    def vy_copy(j, e):
        part = v_all.at[(z + offset_of(j) + NZ) % NZ, c, y]
        return send(part, part, vys.at[j, e - 1], vyr.at[j, e - 1], y_peer(e))

    def kc_copy(j):
        part = k_all.at[(z + offset_of(j) + NZ) % NZ, c]
        return send(part, part, kcs.at[j], kcr.at[j], core_peer)

    def vc_copy(j):
        part = v_all.at[(z + offset_of(j) + NZ) % NZ, c]
        return send(part, part, vcs.at[j], vcr.at[j], core_peer)

    for e in range(1, NX):
        q_copy(0, e).start()
    for e in (1, 7, 2, 6, 3, 5, 4):
        kz_copy(e).start()
    for e in range(1, NY):
        ky_copy(0, e).start()
    for e in range(1, NX):
        q_copy(1, e).start()

    o = o_in[...].astype(f32) * d.astype(f32)
    prod = jnp.concatenate([o[:, h * HD:(h + 1) * HD] for h in range(HEADS)], axis=0)
    high = prod.astype(bf16)
    low = (prod - high.astype(f32)).astype(bf16)
    ones = jnp.ones((8, HD), bf16)
    delta[x] = dot(ones, high, 1, 1) + dot(ones, low, 1, 1)

    row = lax.broadcasted_iota(jnp.int32, (ROWS, HD), 0)
    lane = lax.broadcasted_iota(jnp.int32, (ROWS, HD), 1)

    def start(xx, yy, zz):
        block = (yy * 4 + zz // 2) * 8 + (zz % 2) * 4 + xx
        return p_in[pl.ds(block, 1), 0:1]

    limit = jnp.full((ROWS, HD), 2 ** 30, jnp.int32)
    for xx in range(NX):
        limit = jnp.where(lane == ROWS + xx, start(xx, y, z), limit)

    def mask_keys(n, _):
        j, cc, yy = n // (NC * NY), (n // NY) % NC, n % NY
        zz = (z + offset_of(j) + NZ) % NZ
        at = pl.ds(pl.multiple_of(n * ROWS, ROWS), ROWS)
        k_mask[at, :] = jnp.where(start(x, yy, zz) > limit, HIDDEN, 0.0).astype(bf16)
        return 0

    lax.fori_loop(0, NZ * NC * NY, mask_keys, 0)
    for cc in range(NC):
        at = pl.ds(pl.multiple_of((cc * NY + y) * ROWS, ROWS), ROWS)
        later = (lane < ROWS) & (row + cc * ROWS > lane + c * ROWS)
        k_mask[at, :] = jnp.where(
            later | (start(x, y, z) > limit), HIDDEN, 0.0
        ).astype(bf16)
    for side in range(2):
        for xx in range(NX):
            mine = (lane == ROWS + xx) | ((lane == row) & (x == xx))
            one = jnp.where(mine, 1.0, 0.0).astype(bf16)
            for h in range(4):
                q_mask[pl.ds(side * SIDE + xx * PART + h * ROWS, ROWS), :] = one

    top[...] = jnp.full_like(top, FLOOR)
    total[...] = jnp.zeros_like(total)
    dq_acc[...] = jnp.zeros_like(dq_acc)

    def forward_keys(j, _):
        arrived = (NZ - offset_of(j)) % NZ
        kz_copy(arrived).wait_recv()
        for e in range(1, NY):
            ky_copy(j, e).start()
        return 0

    def share_keys(j):
        for e in range(1, NY):
            ky_copy(j, e).wait_recv()
        kc_copy(j).start()

    lax.fori_loop(1, 3, forward_keys, 0)
    share_keys(0)
    lax.fori_loop(3, 5, forward_keys, 0)
    share_keys(1)
    lax.fori_loop(5, NZ, forward_keys, 0)
    for e in (1, 7, 2, 6, 3, 5, 4):
        vz_copy(e).start()
    for j in range(2, AHEAD):
        share_keys(j)
    for e in range(1, NX):
        q_copy(0, e).wait_recv()

    def forward_values(j):
        @pl.when(j > 0)
        def _():
            vz_copy((NZ - offset_of(j)) % NZ).wait_recv()

        for e in range(1, NY):
            vy_copy(j, e).start()

    def arrive(j):
        @pl.when(j < NZ - AHEAD)
        def _():
            share_keys(j + AHEAD)

        kc_copy(j).wait_recv()

    def statistics(side, prepare):
        cols = pl.ds(side * SIDE, SIDE)
        queries = jnp.concatenate(
            [q_all[side].reshape(SIDE, HD), q_mask[cols, :]], axis=1
        )

        def scores(j, store, t):
            zz = (z + offset_of(j) + NZ) % NZ
            at = pl.ds(pl.multiple_of(j * TILE, TILE), TILE)
            keys = jnp.concatenate([k_all[zz].reshape(TILE, HD), k_mask[at, :]], axis=1)
            raw = dot(keys, queries, 1, 1) * (SCALE * LOG2E)
            store[t, :, cols] = raw
            return jnp.max(raw.reshape(TILE // 8, 8, SIDE), axis=0)

        def sums(store, t, high):
            part = store[t, :, cols].reshape(TILE // 8, 8, SIDE)
            return jnp.sum(jnp.exp2(part - high[None]), axis=0)

        def step(j, store, t, before, s):
            prepare(j)
            high = top[:, cols]
            seen = scores(j, store, t)
            run = total[:, cols] + sums(before, s, high)
            new = jnp.maximum(high, seen)
            total[:, cols] = run * jnp.exp2(high - new)
            top[:, cols] = new

        prepare(jnp.int32(0))
        top[:, cols] = jnp.maximum(top[:, cols], scores(0, s_even, 0))

        def pair(t, _):
            step(2 * t + 1, s_odd, t, s_even, t)

            @pl.when(t < NZ // 2 - 1)
            def _():
                step(2 * t + 2, s_even, t + 1, s_odd, t)

            return 0

        lax.fori_loop(0, NZ // 2, pair, 0)
        high = top[:, cols]
        run = total[:, cols] + sums(s_odd, NZ // 2 - 1, high)
        peak = jnp.max(high, axis=0, keepdims=True)
        mass = jnp.sum(run * jnp.exp2(high - peak), axis=0, keepdims=True)
        mine = jnp.where(mass > 0.0, peak + jnp.log2(mass), FLOOR)
        for n in range(8):
            lse_own[side, n:n + 1, :] = mine[:, n * HD:(n + 1) * HD]
        for e in range(1, NX):
            l_copy(side, e).start()

    def join(side):
        for e in range(1, NX):
            l_copy(side, e).wait_recv()
        parts = [lse_own[side]] + [lse_got[side, e] for e in range(NX - 1)]
        peak = jnp.maximum(jnp.maximum(parts[0], parts[1]), jnp.maximum(parts[2], parts[3]))
        joint = peak + jnp.log2(sum(jnp.exp2(part - peak) for part in parts))
        for n in range(8):
            lse[:, side * SIDE + n * HD:side * SIDE + (n + 1) * HD] = joint[n:n + 1, :]

    statistics(0, arrive)
    for e in range(1, NX):
        q_copy(1, e).wait_recv()
    for e in range(1, NX):
        d_copy(e).start()
        e_copy(e).start()
    statistics(1, forward_values)

    def share_values(j, _):
        for e in range(1, NY):
            vy_copy(j, e).wait_recv()
        vc_copy(j).start()
        return 0

    lax.fori_loop(0, NZ, share_values, 0)
    for e in range(1, NX):
        d_copy(e).wait_recv()
        e_copy(e).wait_recv()
    join(0)

    def pc_copy(i):
        return send(core_send.at[i], core_got.at[i], pcs.at[i], pcr.at[i], core_peer)

    def py_copy(i, e):
        return send(
            y_send.at[i, (y + e) % NY], y_got.at[i, e - 1],
            pys.at[i, e - 1], pyr.at[i, e - 1], y_peer(e),
        )

    def pz_copy(i, e):
        return send(z_send.at[i], z_got.at[e - 1], pzs.at[e - 1], pzr.at[e - 1], z_peer(e))

    def fold_core(i):
        pc_copy(i).wait_recv()
        both = own[i] + core_got[i].astype(f32)
        y_send[i] = both.astype(bf16).reshape(NY, ROWS, 2 * HD)
        for e in range(1, NY):
            py_copy(i, e).start()

    def fold_y(i):
        for e in range(1, NY):
            py_copy(i, e).wait_recv()
        part = y_send[i, y].astype(f32)
        for e in range(NY - 1):
            part = part + y_got[i, e].astype(f32)
        return part

    def send_z(i):
        z_send[i] = fold_y(i).astype(bf16)
        pz_copy(i, (offset_of(NZ - 1 - i) + NZ) % NZ).start()

    def delta_of(side):
        cols = slice(side * PART, (side + 1) * PART)
        return jnp.concatenate([delta[xx, 0:1, cols] for xx in range(NX)], axis=1)


    def ready(i):
        j = NZ - 1 - i
        zz = (z + offset_of(j) + NZ) % NZ

        @pl.when(i >= 2)
        def _():
            fold_core(i - 2)

        @pl.when(i >= 3)
        def _():
            send_z(i - 3)

        vc_copy(j).wait_recv()
        keys = k_all[zz].reshape(TILE, HD)
        values = v_all[zz].reshape(TILE, HD)
        return keys, values

    def terms(keys, values, queries, cots, scored, norm, drop):
        dprob = dot(values, cots, 1, 1)
        probs = jnp.exp2(scored - norm)
        dscore = (probs * (dprob - drop)).astype(bf16)
        half = probs.astype(bf16)
        dv = dot(half, cots, 1, 0)
        dk = dot(dscore, queries, 1, 0)
        return dot(keys, dscore, 0, 0), dk, dv

    def hand_over(i, stage):
        own_rows = pl.ds(pl.multiple_of(c * HALF, HALF), HALF)
        gone_rows = pl.ds(pl.multiple_of((1 - c) * HALF, HALF), HALF)
        core_send[i] = stage[gone_rows, :].astype(bf16)
        pc_copy(i).start()
        own[i] = stage[own_rows, :]

    def grad_side(side, keys, values, store, t, stage):
        cols = pl.ds(side * SIDE, SIDE)
        dq, dk, dv = terms(
            keys, values, q_all[side].reshape(SIDE, HD), d_all[side].reshape(SIDE, HD),
            store[t, :, cols], lse[:, cols], delta_of(side),
        )
        dq_acc[:, cols] += dq
        if side == 0:
            stage[:, 0:HD] = dk * SCALE
            stage[:, HD:2 * HD] = dv
        else:
            stage[:, 0:HD] += dk * SCALE
            stage[:, HD:2 * HD] += dv

    def grad(i, store, t):
        keys, values = ready(i)
        dq, dk, dv = terms(
            keys, values, q_all[...].reshape(COLS, HD), d_all[...].reshape(COLS, HD),
            store[t], lse[...], jnp.concatenate([delta_of(0), delta_of(1)], axis=1),
        )
        dq_acc[...] += dq
        stage[:, 0:HD] = dk * SCALE
        stage[:, HD:2 * HD] = dv
        hand_over(i, stage)

    first, second = ready(0), ready(1)
    grad_side(0, *first, s_odd, NZ // 2 - 1, stage)
    grad_side(0, *second, s_even, NZ // 2 - 1, stage2)
    join(1)
    grad_side(1, *first, s_odd, NZ // 2 - 1, stage)
    hand_over(0, stage)
    grad_side(1, *second, s_even, NZ // 2 - 1, stage2)
    hand_over(1, stage2)

    def grad_pair(t, _):
        grad(2 * t, s_odd, NZ // 2 - 1 - t)

        @pl.when(t < NZ // 2 - 1)
        def _():
            grad(2 * t + 1, s_even, NZ // 2 - 1 - t)

        return 0

    lax.fori_loop(1, NZ // 2, grad_pair, 0)

    keys, values = ready(NZ - 1)

    def last(e, fresh):
        xx = (x + e) % NX
        spans = [
            pl.ds(pl.multiple_of(side * SIDE + xx * PART, PART), PART) for side in range(2)
        ]

        def both(pick, axis):
            return jnp.concatenate([pick(side) for side in range(2)], axis=axis)

        dq, dk, dv = terms(
            keys, values,
            both(lambda side: q_all[side, xx], 0), both(lambda side: d_all[side, xx], 0),
            both(lambda side: s_even[0, :, spans[side]], 1),
            both(lambda side: lse[:, spans[side]], 1), delta[xx, 0:1, :],
        )
        if fresh:
            stage[:, 0:HD] = dk * SCALE
            stage[:, HD:2 * HD] = dv
        else:
            stage[:, 0:HD] += dk * SCALE
            stage[:, HD:2 * HD] += dv
        return both(lambda side: dq_acc[:, spans[side]], 1) + dq

    for e in (2, 1, 3):
        dq_send[e - 1] = last(e, e == 2).astype(bf16)
        g_copy(e).start()
    fold_core(NZ - 2)
    send_z(NZ - 3)
    dq_sum = last(0, False)
    hand_over(NZ - 1, stage)

    fold_core(NZ - 1)
    send_z(NZ - 2)

    for e in range(1, NX):
        g_copy(e).wait_recv()
        dq_sum = dq_sum + dq_got[e - 1].astype(f32)
    dq_rows = jnp.transpose(dq_sum * SCALE).astype(bf16)
    for h in range(HEADS):
        dq_out[:, h * HD:(h + 1) * HD] = dq_rows[h * ROWS:(h + 1) * ROWS, :]

    dq_store = pltpu.make_async_copy(dq_out, dq_hbm, ios.at[0])
    dq_store.start()
    kv_sum = fold_y(NZ - 1)
    for e in range(1, NZ):
        pz_copy(0, e).wait_recv()
        kv_sum = kv_sum + z_got[e - 1].astype(f32)
    dk_out[...] = kv_sum[:, 0:HD].astype(bf16)
    dv_out[...] = kv_sum[:, HD:2 * HD].astype(bf16)
    dk_store = pltpu.make_async_copy(dk_out, dk_hbm, ios.at[1])
    dv_store = pltpu.make_async_copy(dv_out, dv_hbm, ios.at[2])
    dk_store.start()
    dv_store.start()

    for e in range(1, NX):
        q_copy(0, e).wait_send()
        q_copy(1, e).wait_send()
        d_copy(e).wait_send()
        e_copy(e).wait_send()
        l_copy(0, e).wait_send()
        l_copy(1, e).wait_send()
        g_copy(e).wait_send()
    for e in range(1, NZ):
        kz_copy(e).wait_send()
        vz_copy(e).wait_send()
        pz_copy(0, e).wait_send()

    def drain(j, _):
        for e in range(1, NY):
            ky_copy(j, e).wait_send()
            vy_copy(j, e).wait_send()
            py_copy(j, e).wait_send()
        kc_copy(j).wait_send()
        vc_copy(j).wait_send()
        pc_copy(j).wait_send()
        return 0

    lax.fori_loop(0, NZ, drain, 0)
    dq_store.wait()
    dk_store.wait()
    dv_store.wait()


def local(queries, key_vecs, value_vecs, outputs, out_grad, positions):
    blocks = positions.reshape(-1, NC * ROWS)
    hbm = pl.BlockSpec(memory_space=pl.ANY)
    dma = pltpu.SemaphoreType.DMA
    V = pltpu.VMEM
    return pl.pallas_call(
        kernel,
        out_shape=(
            jax.ShapeDtypeStruct((ROWS, HEADS * HD), bf16),
            jax.ShapeDtypeStruct((ROWS, HD), bf16),
            jax.ShapeDtypeStruct((ROWS, HD), bf16),
        ),
        in_specs=[hbm] * 6,
        out_specs=(hbm, hbm, hbm),
        scratch_shapes=[
            V((NX * NY * NZ, NC * ROWS), jnp.int32),
            V((ROWS, HEADS * HD), bf16), V((ROWS, HEADS * HD), bf16), V((ROWS, HEADS * HD), bf16),
            V((ROWS, HEADS * HD), bf16), V((ROWS, HD), bf16), V((ROWS, HD), bf16), dma((6,)),
            V((2, NX, PART, HD), bf16), V((2, NX, PART, HD), bf16),
            V((NX, 8, WIDE), f32),
            V((2, 8, HD), f32), V((2, NX - 1, 8, HD), f32), V((1, COLS), f32),
            V((NZ, NC, NY, ROWS, HD), bf16), V((NZ, NC, NY, ROWS, HD), bf16),
            V((NZ * TILE, HD), bf16), V((COLS, HD), bf16),
            V((NZ // 2, TILE, COLS), f32), V((NZ // 2, TILE, COLS), f32),
            V((8, COLS), f32), V((8, COLS), f32),
            V((HD, COLS), f32), V((NX - 1, HD, WIDE), bf16), V((NX - 1, HD, WIDE), bf16),
            V((TILE, 2 * HD), f32), V((TILE, 2 * HD), f32),
            V((NZ, HALF, 2 * HD), f32),
            V((NZ, HALF, 2 * HD), bf16), V((NZ, HALF, 2 * HD), bf16),
            V((NZ, NY, ROWS, 2 * HD), bf16), V((NZ, NY - 1, ROWS, 2 * HD), bf16),
            V((NZ, ROWS, 2 * HD), bf16), V((NZ - 1, ROWS, 2 * HD), bf16),
        ]
        + [dma((2, NX - 1))] * 2 + [dma((NX - 1,))] * 4 + [dma((2, NX - 1))] * 2 + [dma((NX - 1,))] * 2
        + [dma((NZ - 1,)), dma((NZ - 1,)), dma((NZ, NY - 1)), dma((NZ, NY - 1)), dma((NZ,)), dma((NZ,))] * 2
        + [dma((NZ,)), dma((NZ,)), dma((NZ, NY - 1)), dma((NZ, NY - 1)), dma((NZ - 1,)), dma((NZ - 1,))],
        compiler_params=pltpu.CompilerParams(
            collective_id=0, has_side_effects=True, vmem_limit_bytes=62 * 2**20
        ),
        cost_estimate=pl.CostEstimate(
            flops=12 * COLS * NZ * TILE * HD, bytes_accessed=1 << 20, transcendentals=2 * COLS * NZ * TILE
        ),
    )(blocks, queries, key_vecs, value_vecs, outputs, out_grad)


def solution(mesh):
    rows = P(("pb", "ka"), None)
    return jax.shard_map(
        local,
        mesh=mesh,
        in_specs=(rows, rows, rows, rows, rows, P()),
        out_specs=(rows, rows, rows),
        check_vma=False,
    )
```

time: 83.3 us -> 73.3 us (0.88)
  Pallas kernels: 77.9 us -> 69.5 us
  local copies, waits for them, and re-layouts: 4.52 us -> 2.91 us
    pallas_call x1, Pallas kernels: 77.9 us -> 69.5 us  [local(): pl.pallas_call(kernel, out_shape=(jax.ShapeDtypeStruct((ROWS, HEADS * HD)...]
    slice x1 -> x0, local copies, waits for them, and re-layouts: 1.61 us -> none  [local(): starts = positions[::ROWS]]
where the time goes in v2:
time: 73.3 us; the launch traced here: 73.1 us
  Pallas kernels  69.5 us (95%)
  local copies, waits for them, and re-layouts  2.91 us (4%)
    pallas_call x1, Pallas kernels, local(): pl.pallas_call(kernel, out_shape=(jax.ShapeDtypeStruct((ROWS, HEADS * HD)...  69.5 us
    unnamed x7, local copies, waits for them, and re-layouts  2.91 us

profile of v2, /device:TPU:1, one launch (start us, length us, event | category | flops | bytes accessed | tf_op | source)
XLA Modules:
  0.0 73.1 jit_solution(15974046471215053262)
XLA Ops:
  0.6 69.5 %shard_map.85 = (bf16[64,1024]{1,0:T(8,128)(2,1)}, bf16[64,128]{1,0:T(8,128)(2,1)}, bf16[64,128]{1,0:T(8,128)(2,1)}) custom-call(s32[128,128]{1,0:T(8,128)} %bitcast.1, bf16[64,1024]{1,0:T(8,128)(2,1)} %q_hbm.1, bf16[64,128]{1,0:T(8,128)(2,1)} %k_hbm.1, bf16[64,128]{1,0:T(8,128)(2,1)} %v_hbm.1, bf16[64,1024]{1,0:T(8,128)(2,1)} %o_hbm.1, bf16[64,1024]{1,0:T(8,128)(2,1)} %d_hbm.1), custom_call_target="tpu_custom_call" | custom-call | flops 12884901888 | bytes 1048576 | tf_op jit(solution)/shard_map/pallas_call | solution.py:529
  70.2 0.0 copy-start.1
  70.2 1.6 %copy.12 = bf16[64,1024]{1,0:T(8,128)(2,1)} copy(bf16[64,1024]{1,0:T(8,128)(2,1)} %get-tuple-element.6) | data formatting | bytes 262144
  71.8 0.0 copy-done.1
  71.8 0.0 copy-start
  71.8 0.6 copy.13
  72.4 0.1 copy-done
  72.5 0.6 copy.14
Async XLA Ops:
  70.2 1.6 %copy-start.1 = (bf16[64,128]{1,0:T(8,128)(2,1)S(1)}, bf16[64,128]{1,0:T(8,128)(2,1)}, u32[]{:S(2)}) copy-start(bf16[64,128]{1,0:T(8,128)(2,1)} %get-tuple-element.7) | copy-start | bytes 49156
  71.8 0.7 copy-start

commit v3 on v2

--- a/solution.py
+++ b/solution.py
@@ -160,6 +160,8 @@
         ky_copy(0, e).start()
     for e in range(1, NX):
         q_copy(1, e).start()
+    for e in range(1, NX):
+        d_copy(e).start()
 
     o = o_in[...].astype(f32) * d.astype(f32)
     prod = jnp.concatenate([o[:, h * HD:(h + 1) * HD] for h in range(HEADS)], axis=0)
@@ -167,6 +169,8 @@
     low = (prod - high.astype(f32)).astype(bf16)
     ones = jnp.ones((8, HD), bf16)
     delta[x] = dot(ones, high, 1, 1) + dot(ones, low, 1, 1)
+    for e in range(1, NX):
+        e_copy(e).start()
 
     row = lax.broadcasted_iota(jnp.int32, (ROWS, HD), 0)
     lane = lax.broadcasted_iota(jnp.int32, (ROWS, HD), 1)
@@ -236,10 +240,20 @@
         for e in range(1, NY):
             vy_copy(j, e).start()
 
+    def share_values(j):
+        for e in range(1, NY):
+            vy_copy(NZ - 1 - j, e).wait_recv()
+        vc_copy(NZ - 1 - j).start()
+
     def arrive(j):
         @pl.when(j < NZ - AHEAD)
         def _():
             share_keys(j + AHEAD)
+
+        @pl.when(j >= NZ // 2)
+        def _():
+            forward_values(2 * NZ - 1 - 2 * j)
+            forward_values(2 * NZ - 2 - 2 * j)
 
         kc_copy(j).wait_recv()
 
@@ -305,18 +319,8 @@
     statistics(0, arrive)
     for e in range(1, NX):
         q_copy(1, e).wait_recv()
-    for e in range(1, NX):
-        d_copy(e).start()
-        e_copy(e).start()
-    statistics(1, forward_values)
-
-    def share_values(j, _):
-        for e in range(1, NY):
-            vy_copy(j, e).wait_recv()
-        vc_copy(j).start()
-        return 0
-
-    lax.fori_loop(0, NZ, share_values, 0)
+    statistics(1, share_values)
+
     for e in range(1, NX):
         d_copy(e).wait_recv()
         e_copy(e).wait_recv()
@@ -366,9 +370,9 @@
         def _():
             fold_core(i - 2)
 
-        @pl.when(i >= 3)
+        @pl.when(i >= 4)
         def _():
-            send_z(i - 3)
+            send_z(i - 4)
 
         vc_copy(j).wait_recv()
         keys = k_all[zz].reshape(TILE, HD)
@@ -465,11 +469,12 @@
         dq_send[e - 1] = last(e, e == 2).astype(bf16)
         g_copy(e).start()
     fold_core(NZ - 2)
-    send_z(NZ - 3)
+    send_z(NZ - 4)
     dq_sum = last(0, False)
     hand_over(NZ - 1, stage)
 
     fold_core(NZ - 1)
+    send_z(NZ - 3)
     send_z(NZ - 2)
 
     for e in range(1, NX):

time: 73.3 us -> 69.2 us (0.944)
  Pallas kernels: 69.5 us -> 65.5 us
    pallas_call x1, Pallas kernels: 69.5 us -> 65.5 us  [local(): pl.pallas_call(kernel, out_shape=(jax.ShapeDtypeStruct((ROWS, HEADS * HD)...]
where the time goes in v3:
time: 69.2 us; the launch traced here: 69 us
  Pallas kernels  65.5 us (95%)
  local copies, waits for them, and re-layouts  2.91 us (4%)
    pallas_call x1, Pallas kernels, local(): pl.pallas_call(kernel, out_shape=(jax.ShapeDtypeStruct((ROWS, HEADS * HD)...  65.5 us
    unnamed x7, local copies, waits for them, and re-layouts  2.91 us

profile of v3, /device:TPU:1, one launch (start us, length us, event | category | flops | bytes accessed | tf_op | source)
XLA Modules:
  0.0 69.0 jit_solution(1639967765425730263)
XLA Ops:
  0.6 65.5 %shard_map.85 = (bf16[64,1024]{1,0:T(8,128)(2,1)}, bf16[64,128]{1,0:T(8,128)(2,1)}, bf16[64,128]{1,0:T(8,128)(2,1)}) custom-call(s32[128,128]{1,0:T(8,128)} %bitcast.1, bf16[64,1024]{1,0:T(8,128)(2,1)} %q_hbm.1, bf16[64,128]{1,0:T(8,128)(2,1)} %k_hbm.1, bf16[64,128]{1,0:T(8,128)(2,1)} %v_hbm.1, bf16[64,1024]{1,0:T(8,128)(2,1)} %o_hbm.1, bf16[64,1024]{1,0:T(8,128)(2,1)} %d_hbm.1), custom_call_target="tpu_custom_call" | custom-call | flops 12884901888 | bytes 1048576 | tf_op jit(solution)/shard_map/pallas_call | solution.py:534
  66.1 0.0 copy-start.1
  66.1 1.6 %copy.12 = bf16[64,1024]{1,0:T(8,128)(2,1)} copy(bf16[64,1024]{1,0:T(8,128)(2,1)} %get-tuple-element.6) | data formatting | bytes 262144
  67.7 0.0 copy-done.1
  67.7 0.0 copy-start
  67.7 0.6 copy.13
  68.3 0.1 copy-done
  68.4 0.6 copy.14
Async XLA Ops:
  66.1 1.6 %copy-start.1 = (bf16[64,128]{1,0:T(8,128)(2,1)S(1)}, bf16[64,128]{1,0:T(8,128)(2,1)}, u32[]{:S(2)}) copy-start(bf16[64,128]{1,0:T(8,128)(2,1)} %get-tuple-element.7) | copy-start | bytes 49156
  67.7 0.7 %copy-start = (bf16[64,128]{1,0:T(8,128)(2,1)S(1)}, bf16[64,128]{1,0:T(8,128)(2,1)}, u32[]{:S(2)}) copy-start(bf16[64,128]{1,0:T(8,128)(2,1)} %get-tuple-element.8) | copy-start | bytes 49156

commit v4 on v3

--- a/solution.py
+++ b/solution.py
@@ -16,7 +16,7 @@
 PART = WIDE // 2
 SIDE = COLS // 2
 TILE = NC * NY * ROWS
-AHEAD = 3
+AHEAD = 2
 HALF = NY * ROWS
 
 HIDDEN = -1e30
@@ -163,15 +163,6 @@
     for e in range(1, NX):
         d_copy(e).start()
 
-    o = o_in[...].astype(f32) * d.astype(f32)
-    prod = jnp.concatenate([o[:, h * HD:(h + 1) * HD] for h in range(HEADS)], axis=0)
-    high = prod.astype(bf16)
-    low = (prod - high.astype(f32)).astype(bf16)
-    ones = jnp.ones((8, HD), bf16)
-    delta[x] = dot(ones, high, 1, 1) + dot(ones, low, 1, 1)
-    for e in range(1, NX):
-        e_copy(e).start()
-
     row = lax.broadcasted_iota(jnp.int32, (ROWS, HD), 0)
     lane = lax.broadcasted_iota(jnp.int32, (ROWS, HD), 1)
 
@@ -224,9 +215,19 @@
     share_keys(0)
     lax.fori_loop(3, 5, forward_keys, 0)
     share_keys(1)
-    lax.fori_loop(5, NZ, forward_keys, 0)
     for e in (1, 7, 2, 6, 3, 5, 4):
         vz_copy(e).start()
+
+    o = o_in[...].astype(f32) * d.astype(f32)
+    prod = jnp.concatenate([o[:, h * HD:(h + 1) * HD] for h in range(HEADS)], axis=0)
+    high = prod.astype(bf16)
+    low = (prod - high.astype(f32)).astype(bf16)
+    ones = jnp.ones((8, HD), bf16)
+    delta[x] = dot(ones, high, 1, 1) + dot(ones, low, 1, 1)
+    for e in range(1, NX):
+        e_copy(e).start()
+
+    lax.fori_loop(5, NZ, forward_keys, 0)
     for j in range(2, AHEAD):
         share_keys(j)
     for e in range(1, NX):
@@ -240,10 +241,19 @@
         for e in range(1, NY):
             vy_copy(j, e).start()
 
+    def share_value(j):
+        for e in range(1, NY):
+            vy_copy(j, e).wait_recv()
+        vc_copy(j).start()
+
     def share_values(j):
-        for e in range(1, NY):
-            vy_copy(NZ - 1 - j, e).wait_recv()
-        vc_copy(NZ - 1 - j).start()
+        @pl.when(j >= 2)
+        def _():
+            share_value(NZ + 1 - j)
+
+        @pl.when(j >= NZ - 2)
+        def _():
+            share_value(NZ - 1 - j)
 
     def arrive(j):
         @pl.when(j < NZ - AHEAD)

time: 69.2 us -> 68 us (0.983)
  Pallas kernels: 65.5 us -> 64.3 us
    pallas_call x1, Pallas kernels: 65.5 us -> 64.3 us  [local(): pl.pallas_call(kernel, out_shape=(jax.ShapeDtypeStruct((ROWS, HEADS * HD)...]
where the time goes in v4:
time: 68 us; the launch traced here: 67.9 us
  Pallas kernels  64.3 us (95%)
  local copies, waits for them, and re-layouts  2.91 us (4%)
    pallas_call x1, Pallas kernels, local(): pl.pallas_call(kernel, out_shape=(jax.ShapeDtypeStruct((ROWS, HEADS * HD)...  64.3 us
    unnamed x7, local copies, waits for them, and re-layouts  2.91 us

profile of v4, /device:TPU:1, one launch (start us, length us, event | category | flops | bytes accessed | tf_op | source)
XLA Modules:
  0.0 67.9 jit_solution(4423639008014092550)
XLA Ops:
  0.6 64.3 %shard_map.85 = (bf16[64,1024]{1,0:T(8,128)(2,1)}, bf16[64,128]{1,0:T(8,128)(2,1)}, bf16[64,128]{1,0:T(8,128)(2,1)}) custom-call(s32[128,128]{1,0:T(8,128)} %bitcast.1, bf16[64,1024]{1,0:T(8,128)(2,1)} %q_hbm.1, bf16[64,128]{1,0:T(8,128)(2,1)} %k_hbm.1, bf16[64,128]{1,0:T(8,128)(2,1)} %v_hbm.1, bf16[64,1024]{1,0:T(8,128)(2,1)} %o_hbm.1, bf16[64,1024]{1,0:T(8,128)(2,1)} %d_hbm.1), custom_call_target="tpu_custom_call" | custom-call | flops 12884901888 | bytes 1048576 | tf_op jit(solution)/shard_map/pallas_call | solution.py:544
  64.9 0.0 copy-start.1
  64.9 1.6 %copy.12 = bf16[64,1024]{1,0:T(8,128)(2,1)} copy(bf16[64,1024]{1,0:T(8,128)(2,1)} %get-tuple-element.6) | data formatting | bytes 262144
  66.5 0.0 copy-done.1
  66.5 0.0 copy-start
  66.5 0.6 copy.13
  67.1 0.1 copy-done
  67.2 0.6 copy.14
Async XLA Ops:
  64.9 1.6 %copy-start.1 = (bf16[64,128]{1,0:T(8,128)(2,1)S(1)}, bf16[64,128]{1,0:T(8,128)(2,1)}, u32[]{:S(2)}) copy-start(bf16[64,128]{1,0:T(8,128)(2,1)} %get-tuple-element.7) | copy-start | bytes 49156
  66.5 0.7 %copy-start = (bf16[64,128]{1,0:T(8,128)(2,1)S(1)}, bf16[64,128]{1,0:T(8,128)(2,1)}, u32[]{:S(2)}) copy-start(bf16[64,128]{1,0:T(8,128)(2,1)} %get-tuple-element.8) | copy-start | bytes 49156

commit v5 on v4

--- a/solution.py
+++ b/solution.py
@@ -97,14 +97,12 @@
     ]
     for load in loads:
         load.start()
-    for load in loads:
+    for load in loads[:2]:
         load.wait()
     q = q_in[...]
-    d = d_in[...]
     for h in range(HEADS):
         rows = pl.ds((h % 4) * ROWS, ROWS)
         q_all[h // 4, x, rows, :] = q[:, h * HD:(h + 1) * HD]
-        d_all[h // 4, x, rows, :] = d[:, h * HD:(h + 1) * HD]
 
     pl.semaphore_wait(barrier, len(peers))
 
@@ -160,6 +158,12 @@
         ky_copy(0, e).start()
     for e in range(1, NX):
         q_copy(1, e).start()
+    for load in loads[2:]:
+        load.wait()
+    d = d_in[...]
+    for h in range(HEADS):
+        rows = pl.ds((h % 4) * ROWS, ROWS)
+        d_all[h // 4, x, rows, :] = d[:, h * HD:(h + 1) * HD]
     for e in range(1, NX):
         d_copy(e).start()
 
@@ -389,11 +393,14 @@
         values = v_all[zz].reshape(TILE, HD)
         return keys, values
 
-    def terms(keys, values, queries, cots, scored, norm, drop):
+    def halves(values, cots, scored, norm, drop):
         dprob = dot(values, cots, 1, 1)
         probs = jnp.exp2(scored - norm)
         dscore = (probs * (dprob - drop)).astype(bf16)
-        half = probs.astype(bf16)
+        return dscore, probs.astype(bf16)
+
+    def terms(keys, values, queries, cots, scored, norm, drop):
+        dscore, half = halves(values, cots, scored, norm, drop)
         dv = dot(half, cots, 1, 0)
         dk = dot(dscore, queries, 1, 0)
         return dot(keys, dscore, 0, 0), dk, dv
@@ -461,23 +468,28 @@
         def both(pick, axis):
             return jnp.concatenate([pick(side) for side in range(2)], axis=axis)
 
-        dq, dk, dv = terms(
-            keys, values,
-            both(lambda side: q_all[side, xx], 0), both(lambda side: d_all[side, xx], 0),
-            both(lambda side: s_even[0, :, spans[side]], 1),
+        queries = both(lambda side: q_all[side, xx], 0)
+        cots = both(lambda side: d_all[side, xx], 0)
+        dscore, half = halves(
+            values, cots, both(lambda side: s_even[0, :, spans[side]], 1),
             both(lambda side: lse[:, spans[side]], 1), delta[xx, 0:1, :],
         )
+        dq = both(lambda side: dq_acc[:, spans[side]], 1) + dot(keys, dscore, 0, 0)
+        if e > 0:
+            dq_send[e - 1] = dq.astype(bf16)
+            g_copy(e).start()
+        dv = dot(half, cots, 1, 0)
+        dk = dot(dscore, queries, 1, 0)
         if fresh:
             stage[:, 0:HD] = dk * SCALE
             stage[:, HD:2 * HD] = dv
         else:
             stage[:, 0:HD] += dk * SCALE
             stage[:, HD:2 * HD] += dv
-        return both(lambda side: dq_acc[:, spans[side]], 1) + dq
+        return dq
 
     for e in (2, 1, 3):
-        dq_send[e - 1] = last(e, e == 2).astype(bf16)
-        g_copy(e).start()
+        last(e, e == 2)
     fold_core(NZ - 2)
     send_z(NZ - 4)
     dq_sum = last(0, False)

time: 68 us -> 67.8 us (level)
  no operation moved by 1% of the time
where the time goes in v5:
time: 67.8 us; the launch traced here: 67.6 us
  Pallas kernels  64.1 us (95%)
  local copies, waits for them, and re-layouts  2.91 us (4%)
    pallas_call x1, Pallas kernels, local(): pl.pallas_call(kernel, out_shape=(jax.ShapeDtypeStruct((ROWS, HEADS * HD)...  64.1 us
    unnamed x7, local copies, waits for them, and re-layouts  2.91 us

profile of v5, /device:TPU:1, one launch (start us, length us, event | category | flops | bytes accessed | tf_op | source)
XLA Modules:
  0.0 67.6 jit_solution(9881767146612423898)
XLA Ops:
  0.6 64.1 %shard_map.85 = (bf16[64,1024]{1,0:T(8,128)(2,1)}, bf16[64,128]{1,0:T(8,128)(2,1)}, bf16[64,128]{1,0:T(8,128)(2,1)}) custom-call(s32[128,128]{1,0:T(8,128)} %bitcast.1, bf16[64,1024]{1,0:T(8,128)(2,1)} %q_hbm.1, bf16[64,128]{1,0:T(8,128)(2,1)} %k_hbm.1, bf16[64,128]{1,0:T(8,128)(2,1)} %v_hbm.1, bf16[64,1024]{1,0:T(8,128)(2,1)} %o_hbm.1, bf16[64,1024]{1,0:T(8,128)(2,1)} %d_hbm.1), custom_call_target="tpu_custom_call" | custom-call | flops 12884901888 | bytes 1048576 | tf_op jit(solution)/shard_map/pallas_call | solution.py:556
  64.7 0.0 copy-start.1
  64.7 1.6 %copy.12 = bf16[64,1024]{1,0:T(8,128)(2,1)} copy(bf16[64,1024]{1,0:T(8,128)(2,1)} %get-tuple-element.6) | data formatting | bytes 262144
  66.3 0.0 copy-done.1
  66.3 0.0 copy-start
  66.3 0.6 copy.13
  66.9 0.1 copy-done
  67.0 0.6 copy.14
Async XLA Ops:
  64.7 1.6 %copy-start.1 = (bf16[64,128]{1,0:T(8,128)(2,1)S(1)}, bf16[64,128]{1,0:T(8,128)(2,1)}, u32[]{:S(2)}) copy-start(bf16[64,128]{1,0:T(8,128)(2,1)} %get-tuple-element.7) | copy-start | bytes 49156
  66.3 0.7 %copy-start = (bf16[64,128]{1,0:T(8,128)(2,1)S(1)}, bf16[64,128]{1,0:T(8,128)(2,1)}, u32[]{:S(2)}) copy-start(bf16[64,128]{1,0:T(8,128)(2,1)} %get-tuple-element.8) | copy-start | bytes 49156
